TPU v7x, 256 devices: a whole 4x4x8 slice. The times are simulated.
256 devices in a mesh: seg: 8 (over y, core), coil: 16 (over x, z_lo), tile: 2 (over z_hi).
Axes of the slice: x: 4, y: 4, z: 8 (z_hi: 2, z_lo: 4; z = z_hi * 4 + z_lo), core: 2. Of those that a mesh axis runs over, the one named last changes fastest.
Arguments:
- right_side: float32 [1024, 128], P(('seg', 'coil', 'tile')), may hold values from -6 to 6
- sensitivity: float32 [32, 1024, 128], P('coil'), may hold values from -0.75 to 0.75
- field_map: float32 [1024, 64], replicated, may hold values from -12 to 12
- seg_map: int32 [1024, 4], replicated, may hold values from 0 to 23, all different within a row; in each aligned block of 1024 rows (0 to 1023, 1024 to 2047, ...) at most 256 rows name the same one
- sample_rows: int32 [24, 2048], P('seg', 'tile'), may hold values from 0 to 1023
- density: float32 [24, 2048, 64], P('seg', 'tile'), may hold values from 0.25 to 4
- step_alpha: float32 [2], replicated, may hold values from 0.15 to 0.35
- step_beta: float32 [2], replicated, may hold values from 0.1 to 0.5
Outputs:
- solution_field: float32 [1024, 128], P(('seg', 'coil', 'tile'))
- residual: float32 [1024, 128], P(('seg', 'coil', 'tile'))
Inputs may be any that keep to these rules, and one draw needn't show every extreme that they name: `seg_map`: each row names 4 different segments; each segment is named by at most 256 tiles, a bound that some block reaches.
All inputs are finite; a program needn't handle non-finite values.
Results may differ from a plain program's by a relative error of at most 0.0001.
Values sent between devices are 32-bit elements; how exact they have to be, the bound alone decides.
No kernel may reach another device: no remote copies, remote signals or barrier semaphores. Data moves between devices by JAX's collectives and lax.ppermute only.
A program may use at most 128 MiB of HBM per device.

v0:
```python
import math
import jax
import jax.numpy as jnp
from jax import lax
from jax.sharding import PartitionSpec as P

SEGS = 24
TV = 64
ITERS = 2
CAP = 256
ridge_weight = 0.25
highest = lax.Precision.HIGHEST


def tile_list(seg_map, segment, slots):
    tile_count = seg_map.shape[0]
    is_member = jnp.any(seg_map == segment, axis=1).astype(jnp.int32)
    live_count = jnp.sum(is_member)
    sort_keys = (1 - is_member) * tile_count + jnp.arange(tile_count, dtype=jnp.int32)
    sorted_tiles = jnp.argsort(sort_keys)
    listed = sorted_tiles[:slots]
    valid_slots = (jnp.arange(slots, dtype=jnp.int32) < live_count).astype(jnp.float32)
    return (listed, valid_slots)


def row_tables(rows_here, listed, valid_slots, tile_count):
    product = rows_here[:, None] * listed[None, :] % tile_count
    angles = product.astype(jnp.float32) * jnp.float32(2.0 * math.pi / tile_count)
    slot_scale = valid_slots[None, :] / jnp.float32(math.sqrt(tile_count))
    return (jnp.cos(angles) * slot_scale, -jnp.sin(angles) * slot_scale)


def column_tables(voxels):
    steps_here = jnp.arange(voxels, dtype=jnp.int32)
    product = steps_here[:, None] * steps_here[None, :] % voxels
    angles = product.astype(jnp.float32) * jnp.float32(2.0 * math.pi / voxels)
    norm_factor = jnp.float32(1.0 / math.sqrt(voxels))
    return (jnp.cos(angles) * norm_factor, -jnp.sin(angles) * norm_factor)


def segment_normal(
    dir_rows, sens_rows, field_rows, seg_time, row_cos, row_sin, col_cos, col_sin, weights
):
    voxels = field_rows.shape[1]
    phase_angle = field_rows * seg_time
    phase_real = jnp.cos(phase_angle)
    phase_imag = -jnp.sin(phase_angle)
    dir_real = dir_rows[:, :voxels]
    dir_imag = dir_rows[:, voxels:]
    image_real = phase_real * dir_real - phase_imag * dir_imag
    image_imag = phase_real * dir_imag + phase_imag * dir_real
    sens_real = sens_rows[..., :voxels]
    sens_imag = sens_rows[..., voxels:]
    coil_real = sens_real * image_real - sens_imag * image_imag
    coil_imag = sens_real * image_imag + sens_imag * image_real
    grid_real = jnp.einsum("mn,cnv->cmv", row_cos, coil_real, precision=highest) - jnp.einsum(
        "mn,cnv->cmv", row_sin, coil_imag, precision=highest
    )
    grid_imag = jnp.einsum("mn,cnv->cmv", row_cos, coil_imag, precision=highest) + jnp.einsum(
        "mn,cnv->cmv", row_sin, coil_real, precision=highest
    )
    kspace_real = jnp.einsum("cmv,vj->cmj", grid_real, col_cos, precision=highest) - jnp.einsum(
        "cmv,vj->cmj", grid_imag, col_sin, precision=highest
    )
    kspace_imag = jnp.einsum("cmv,vj->cmj", grid_real, col_sin, precision=highest) + jnp.einsum(
        "cmv,vj->cmj", grid_imag, col_cos, precision=highest
    )
    kspace_real = kspace_real * weights[None]
    kspace_imag = kspace_imag * weights[None]
    back_real = jnp.einsum("cmj,jv->cmv", kspace_real, col_cos, precision=highest) + jnp.einsum(
        "cmj,jv->cmv", kspace_imag, col_sin, precision=highest
    )
    back_imag = jnp.einsum("cmj,jv->cmv", kspace_imag, col_cos, precision=highest) - jnp.einsum(
        "cmj,jv->cmv", kspace_real, col_sin, precision=highest
    )
    rows_real = jnp.einsum("mn,cmv->cnv", row_cos, back_real, precision=highest) + jnp.einsum(
        "mn,cmv->cnv", row_sin, back_imag, precision=highest
    )
    rows_imag = jnp.einsum("mn,cmv->cnv", row_cos, back_imag, precision=highest) - jnp.einsum(
        "mn,cmv->cnv", row_sin, back_real, precision=highest
    )
    summed_real = jnp.sum(sens_real * rows_real + sens_imag * rows_imag, axis=0)
    summed_imag = jnp.sum(sens_real * rows_imag - sens_imag * rows_real, axis=0)
    result_real = phase_real * summed_real + phase_imag * summed_imag
    result_imag = phase_real * summed_imag - phase_imag * summed_real
    return jnp.concatenate([result_real, result_imag], axis=1)


def gather_direction(own_tiles):
    return lax.all_gather(own_tiles, ("seg", "coil", "tile"), axis=0, tiled=True)


def shards(
    right_side, sensitivity, field_map, seg_map, sample_rows, density, step_alpha, step_beta
):
    seg_local = sample_rows.shape[0]
    tile_count = field_map.shape[0]
    first_segment = lax.axis_index("seg") * seg_local
    col_cos, col_sin = column_tables(TV)
    prepared = []
    for local_seg in range(seg_local):
        segment = first_segment + local_seg
        listed, valid_slots = tile_list(seg_map, segment, CAP)
        row_cos, row_sin = row_tables(sample_rows[local_seg], listed, valid_slots, tile_count)
        seg_time = (segment.astype(jnp.float32) + 0.5) / jnp.float32(SEGS)
        prepared.append(
            (
                listed,
                row_cos,
                row_sin,
                seg_time,
                sensitivity[:, listed],
                field_map[listed],
                density[local_seg],
            )
        )
    direction = right_side
    solution_field = jnp.zeros_like(right_side)
    residual = right_side
    for step in range(ITERS):
        gathered = gather_direction(direction)
        partial_value = jnp.zeros(gathered.shape, jnp.float32)
        for (
            local_listed,
            local_row_cos,
            local_row_sin,
            local_seg_time,
            sens_rows,
            field_rows,
            weights,
        ) in prepared:
            contrib = segment_normal(
                gathered[local_listed],
                sens_rows,
                field_rows,
                local_seg_time,
                local_row_cos,
                local_row_sin,
                col_cos,
                col_sin,
                weights,
            )
            partial_value = partial_value.at[local_listed].add(contrib)
        image = (
            lax.psum_scatter(
                partial_value, ("seg", "coil", "tile"), scatter_dimension=0, tiled=True
            )
            + ridge_weight * direction
        )
        solution_field = solution_field + step_alpha[step] * direction
        residual = residual - step_alpha[step] * image
        direction = residual + step_beta[step] * direction
    return (solution_field, residual)


def solution(mesh):
    placed = (
        P(("seg", "coil", "tile"), None),
        P("coil", None, None),
        P(),
        P(),
        P("seg", "tile"),
        P("seg", "tile", None),
        P(),
        P(),
    )
    return jax.shard_map(
        shards,
        mesh=mesh,
        in_specs=placed,
        out_specs=(P(("seg", "coil", "tile"), None), P(("seg", "coil", "tile"), None)),
        check_vma=False,
    )
```

profile of v0, /device:TPU:2, one launch (start us, length us, event | category | flops | bytes accessed | tf_op | source)
XLA Modules:
  0.0 2122.0 jit_solution(18167346693493669759)
XLA Ops:
  16.2 626.4 %all-gather = f32[256,4,128]{2,1,0:T(4,128)S(1)} all-gather(f32[1,4,128]{2,1,0:T(4,128)S(1)} %bitcast.389), channel_id=1, replica_groups=mesh['seg'=8,'coil'=16,'tile'=2] {'seg','coil','tile'}, dimensions={0}, use_global_device_ids=true | all-gather | bytes 526336 | tf_op jit(solution)/shard_map/all_gather | solution.py:90
  646.4 4.9 fusion.67
  651.2 6.3 fusion.65
  657.6 4.9 fusion.4
  679.7 6.5 fusion.89
  686.2 4.9 fusion.91
  691.1 4.9 fusion.2
  710.9 6.1 fusion.113
  717.1 4.9 fusion.115
  722.0 4.9 fusion
  730.1 5.3 fusion.5
  739.3 4.7 fusion.63
  749.3 4.6 fusion.30
  753.9 4.8 subtract_reduce_fusion.3
  760.0 4.9 fusion.3
  774.7 4.5 fusion.85
  779.3 4.8 fusion.32
  784.1 4.6 subtract_reduce_fusion.4
  789.9 6.7 fusion.1
  806.0 4.9 fusion.109
  811.0 4.6 fusion.34
  815.6 4.6 subtract_reduce_fusion.5
  829.0 247.1 %all-reduce.5.cloned.1.call-done = f32[1024,128]{1,0:T(8,128)} async-done(((f32[1024,128]{1,0:T(8,128)}), f32[1024,128]{1,0:T(8,128)}) %all-reduce.5.cloned.1.call-update) | async-done | bytes 524304
  1078.1 621.9 %all-gather.1 = f32[256,4,128]{2,1,0:T(4,128)S(1)} all-gather(f32[1,4,128]{2,1,0:T(4,128)S(1)} %fusion.641), channel_id=1, replica_groups=mesh['seg'=8,'coil'=16,'tile'=2] {'seg','coil','tile'}, dimensions={0}, use_global_device_ids=true | all-gather | bytes 526336 | tf_op jit(solution)/shard_map/all_gather | solution.py:90
  1701.9 6.4 fusion.57
  1708.3 4.9 fusion.59
  1713.2 4.9 fusion.10
  1723.1 6.2 fusion.81
  1729.3 4.9 fusion.83
  1734.2 4.9 fusion.8
  1744.2 6.2 fusion.105
  1750.4 4.9 fusion.107
  1755.3 4.9 fusion.6
  1762.1 5.3 fusion.11
  1771.5 4.7 fusion.55
  1776.9 4.5 fusion.53
  1781.5 4.6 fusion.24
  1786.1 5.6 subtract_reduce_fusion
  1792.9 6.5 fusion.9
  1808.8 4.7 fusion.77
  1813.5 4.6 fusion.26
  1818.1 4.6 subtract_reduce_fusion.1
  1824.0 6.9 fusion.7
  1834.6 4.5 fusion.103
  1839.9 4.7 fusion.101
  1844.6 4.6 fusion.28
  1849.3 4.6 subtract_reduce_fusion.2
  1861.3 250.4 %all-reduce.7.cloned.1.call-done = f32[1024,128]{1,0:T(8,128)} async-done(((f32[1024,128]{1,0:T(8,128)}), f32[1024,128]{1,0:T(8,128)}) %all-reduce.7.cloned.1.call-update) | async-done | bytes 524304
  (326 shorter events, 133.7 us)
Async XLA Ops:
  7.2 636.5 %copy-start = (f32[2,1024,128]{2,1,0:T(8,128)S(1)}, f32[2,1024,128]{2,1,0:T(8,128)}, u32[]{:S(2)}) copy-start(f32[2,1024,128]{2,1,0:T(8,128)} %param.9) | copy-start | bytes 3145732
  7.2 1068.9 %all-reduce.5.cloned.1.call-start = ((), (), s32[]{:S(2)}) async-start(), calls=%async_computation | async-start | bytes 1048576
  13.7 643.9 %copy-start.67 = (s32[256]{0:T(256)}, s32[256]{0:T(256)S(1)}, u32[]{:S(2)}) copy-start(s32[256]{0:T(256)S(1)} %get-tuple-element.67) | copy-start | bytes 3076
  644.8 12.8 copy-start.17
  645.5 12.1 copy-start.77
  646.1 11.5 copy-start.60
  646.4 11.3 copy-start.25
  646.4 11.3 copy-start.27
  669.0 1.5 copy-start.50
  673.0 3.3 copy-start.14
  677.1 1.9 copy-start.19
  677.8 13.3 copy-start.81
  679.0 12.1 copy-start.29
  679.0 12.1 copy-start.31
  706.0 1.6 copy-start.51
  708.8 1.1 copy-start.11
  709.2 12.8 copy-start.21
  709.9 12.0 copy-start.84
  710.2 11.8 copy-start.37
  710.2 11.8 copy-start.39
  728.5 1.6 copy-start.18
  728.5 1.6 copy-start.26
  728.5 1.6 copy-start.28
  728.5 1.6 copy-start.61
  728.5 1.6 copy-start.68
  728.5 1.6 copy-start.78
  728.5 1.6 copy-start.87
  730.1 5.4 copy-start.15
  753.9 5.3 copy-start.88
  760.0 5.0 copy-start.4
  765.7 1.0 copy-start.3
  789.9 6.8 copy-start.6
  797.4 1.0 copy-start.5
  815.6 4.6 copy-start.12
  827.6 1284.1 %all-reduce.7.cloned.1.call-start = ((), (), s32[]{:S(2)}) async-start(), calls=%async_computation.1 | async-start | bytes 1048576
  1700.0 1.3 copy-start.79
  1701.3 11.9 copy-start.45
  1701.3 11.9 copy-start.47
  1723.1 11.1 copy-start.41
  1723.1 11.1 copy-start.43
  1743.8 11.5 copy-start.33
  1743.8 11.5 copy-start.35
  1761.0 1.1 copy-start.89
  1762.1 5.3 copy-start.10
  1768.2 1.0 copy-start.9
  1792.9 6.5 copy-start.8
  1849.3 4.6 copy-start.13
  1856.2 2.2 copy-start.16
  (44 other events, 36.6 us)
Sparse Core Ops, SparseCore 0:
  827.7 248.2 all-reduce.4
  1861.4 250.2 all-reduce.6
where the time goes:
time: 2130 us; the launch traced here: 2120 us
  blocking collectives  1250 us (59%)
  waiting for transfers between devices  498 us (23%)
  matrix products  287 us (13%)
  other arithmetic  40 us (2%)
  local copies, waits for them, and re-layouts  32.9 us (2%)
    all_gather x2, blocking collectives, gather_direction(): lax.all_gather(own_tiles, ('seg', 'coil', 'tile'), axis=0, tiled=True)  1250 us
    unnamed x4, waiting for transfers between devices  498 us
  transfers between devices with their start and end apart: 2, of which 2 were waited for; matrix products, arithmetic and copies ran while one was open for 0% of the time, Pallas kernels for 0%

commit v1 on v0

--- a/solution.py
+++ b/solution.py
@@ -87,7 +87,15 @@
 
 
 def gather_direction(own_tiles):
-    return lax.all_gather(own_tiles, ("seg", "coil", "tile"), axis=0, tiled=True)
+    return jnp.concatenate(
+        lax.all_to_all(
+            jnp.stack([own_tiles] * lax.axis_size(("seg", "coil", "tile"))),
+            ("seg", "coil", "tile"),
+            0,
+            0,
+        ),
+        axis=0,
+    )
 
 
 def shards(

time: 2130 us -> 931 us (0.44)
  blocking collectives: 1250 us -> 30.2 us
    all_gather x2 -> x0, blocking collectives: 1250 us -> none  [gather_direction(): lax.all_gather(own_tiles, ('seg', 'coil', 'tile'), axis=0, tiled=True)]
    all_to_all x0 -> x1, blocking collectives: none -> 30.2 us  [gather_direction(): lax.all_to_all(jnp.stack([own_tiles] * lax.axis_size(('seg', 'coil', 'til...]
  transfers between devices with their start and end apart: 2 -> 3, of which waited for: 2 -> 2; matrix products, arithmetic and copies ran while one was open for 0% -> 3% of each run, Pallas kernels for 0% -> 0%
where the time goes in v1:
time: 931 us; the launch traced here: 922 us
  waiting for transfers between devices  500 us (54%)
  matrix products  289 us (31%)
  other arithmetic  41.2 us (4%)
  local copies, waits for them, and re-layouts  30.8 us (3%)
  blocking collectives  30.2 us (3%)
  between operations  16.5 us (2%)
  starting transfers between devices  14.8 us (2%)
    unnamed x4, waiting for transfers between devices  500 us
    dot_general x6, matrix products, segment_normal(): jnp.einsum('mn,cnv->cmv', row_cos, coil_imag, precision=highest)  38 us
    dot_general x6, matrix products, segment_normal(): jnp.einsum('mn,cnv->cmv', row_sin, coil_real, precision=highest)  37.1 us
    all_to_all x1, blocking collectives, gather_direction(): lax.all_to_all(jnp.stack([own_tiles] * lax.axis_size(('seg', 'coil', 'til...  30.2 us
    dot_general x6, matrix products, segment_normal(): jnp.einsum('mn,cnv->cmv', row_sin, coil_imag, precision=highest)  29.6 us
    dot_general x6, matrix products, segment_normal(): jnp.einsum('mn,cmv->cnv', row_sin, back_imag, precision=highest)  29.4 us
    dot_general x6, matrix products, segment_normal(): jnp.einsum('mn,cnv->cmv', row_cos, coil_real, precision=highest)  29.2 us
    dot_general x6, matrix products, segment_normal(): jnp.einsum('mn,cmv->cnv', row_cos, back_imag, precision=highest)  28.2 us
  transfers between devices with their start and end apart: 3, of which 2 were waited for; matrix products, arithmetic and copies ran while one was open for 3% of the time, Pallas kernels for 0%

profile of v1, /device:TPU:2, one launch (start us, length us, event | category | flops | bytes accessed | tf_op | source)
XLA Modules:
  0.0 922.3 jit_solution(7805666540122124228)
XLA Ops:
  8.8 14.7 %all-to-all-start = ((f32[256,4,128]{2,1,0:T(4,128)}), f32[256,4,128]{2,1,0:T(4,128)S(1)}, u32[]{:S(2)}, u32[]{:S(2)}) async-start(f32[256,4,128]{2,1,0:T(4,128)} %stack.4), calls=%async_computation | async-start | bytes 1048576 | tf_op jit(solution)/shard_map/all_to_all | solution.py:91
  55.5 4.9 fusion.67
  60.4 6.4 fusion.65
  66.8 4.9 fusion.4
  76.8 6.6 fusion.89
  83.4 4.9 fusion.91
  88.3 4.9 fusion.2
  98.6 6.2 fusion.113
  104.7 4.9 fusion.115
  109.6 4.9 fusion
  116.5 5.3 fusion.5
  125.9 4.7 fusion.63
  131.4 4.5 fusion.61
  136.0 4.6 fusion.30
  140.6 5.6 subtract_reduce_fusion.3
  146.6 6.5 fusion.3
  157.3 4.5 fusion.87
  162.6 4.7 fusion.85
  167.3 4.6 fusion.32
  171.9 4.6 subtract_reduce_fusion.4
  177.7 7.0 fusion.1
  193.8 4.7 fusion.109
  198.5 4.6 fusion.34
  203.1 4.6 subtract_reduce_fusion.5
  216.5 252.9 %all-reduce.5.cloned.1.call-done = f32[1024,128]{1,0:T(8,128)} async-done(((f32[1024,128]{1,0:T(8,128)}), f32[1024,128]{1,0:T(8,128)}) %all-reduce.5.cloned.1.call-update) | async-done | bytes 524304
  472.6 30.2 %all_to_all.10 = f32[256,4,128]{2,1,0:T(4,128)S(1)} all-to-all(f32[256,4,128]{2,1,0:T(4,128)S(1)} %stack.5), channel_id=1, replica_groups=mesh['seg'=8,'coil'=16,'tile'=2] {'seg','coil','tile'}, dimensions={0} | all-to-all | bytes 1048576 | tf_op jit(solution)/shard_map/all_to_all | solution.py:91
  505.8 6.5 fusion.57
  512.3 4.9 fusion.59
  517.2 4.9 fusion.10
  527.7 6.2 fusion.81
  533.8 4.9 fusion.83
  538.7 4.9 fusion.8
  549.4 6.1 fusion.105
  555.6 4.9 fusion.107
  560.5 4.9 fusion.6
  567.4 5.1 fusion.11
  576.6 4.9 fusion.55
  586.8 4.6 fusion.24
  591.4 5.4 subtract_reduce_fusion
  597.2 6.5 fusion.9
  613.2 4.9 fusion.77
  618.1 4.6 fusion.26
  622.7 4.6 subtract_reduce_fusion.1
  628.5 6.6 fusion.7
  644.2 4.7 fusion.101
  649.0 4.6 fusion.28
  653.6 4.6 subtract_reduce_fusion.2
  665.7 246.8 %all-reduce.7.cloned.1.call-done = f32[1024,128]{1,0:T(8,128)} async-done(((f32[1024,128]{1,0:T(8,128)}), f32[1024,128]{1,0:T(8,128)}) %all-reduce.7.cloned.1.call-update) | async-done | bytes 524304
  (327 shorter events, 132.3 us)
Async XLA Ops:
  7.2 23.7 %copy-start = (f32[2,1024,128]{2,1,0:T(8,128)S(1)}, f32[2,1024,128]{2,1,0:T(8,128)}, u32[]{:S(2)}) copy-start(f32[2,1024,128]{2,1,0:T(8,128)} %param.9) | copy-start | bytes 3145732
  8.8 21.1 %copy-start.15 = (f32[1024,64]{0,1:T(8,128)S(1)}, f32[1024,64]{0,1:T(8,128)}, u32[]{:S(2)}) copy-start(f32[1024,64]{0,1:T(8,128)} %param.10) | copy-start | bytes 786436
  8.8 44.5 %all-to-all-start = ((f32[256,4,128]{2,1,0:T(4,128)}), f32[256,4,128]{2,1,0:T(4,128)S(1)}, u32[]{:S(2)}, u32[]{:S(2)}) async-start(f32[256,4,128]{2,1,0:T(4,128)} %stack.4), calls=%async_computation | async-start | bytes 1048576 | tf_op jit(solution)/shard_map/all_to_all | solution.py:91
  23.5 445.8 %all-reduce.5.cloned.1.call-start = ((), (), s32[]{:S(2)}) async-start(), calls=%async_computation.2 | async-start | bytes 1048576
  29.9 0.9 copy-start.48
  36.8 38.0 %copy-start.47 = (s32[1024]{0:T(1024)}, s32[1024]{0:T(1024)S(1)}, u32[]{:S(2)}) copy-start(s32[1024]{0:T(1024)S(1)} %pad_clamp_fusion.1) | copy-start | bytes 12292
  44.7 51.7 %copy-start.46 = (s32[1024]{0:T(1024)}, s32[1024]{0:T(1024)S(1)}, u32[]{:S(2)}) copy-start(s32[1024]{0:T(1024)S(1)} %pad_clamp_fusion.2) | copy-start | bytes 12292
  46.5 7.9 copy-start.11
  47.6 124.3 %copy-start.18 = (f32[256,2,128]{0,2,1:T(8,128)}, f32[256,2,128]{0,2,1:T(8,128)S(1)}, u32[]{:S(2)}) copy-start(f32[256,2,128]{0,2,1:T(8,128)S(1)} %copy.93) | copy-start | bytes 786436
  47.7 3.8 copy-start.49
  47.8 61.8 %copy-start.16 = (f32[256,2,128]{0,2,1:T(8,128)}, f32[256,2,128]{0,2,1:T(8,128)S(1)}, u32[]{:S(2)}) copy-start(f32[256,2,128]{0,2,1:T(8,128)S(1)} %copy.87) | copy-start | bytes 786436
  54.5 1.0 copy-start.20
  54.5 0.9 copy-start.83
  54.7 12.0 %copy-start.36 = (f32[256,64]{0,1:T(8,128)}, f32[256,64]{0,1:T(8,128)S(1)}, u32[]{:S(2)}) copy-start(f32[256,64]{0,1:T(8,128)S(1)} %get-tuple-element.42) | copy-start | bytes 196612
  54.7 12.0 %copy-start.38 = (f32[256,64]{0,1:T(8,128)}, f32[256,64]{0,1:T(8,128)S(1)}, u32[]{:S(2)}) copy-start(f32[256,64]{0,1:T(8,128)S(1)} %get-tuple-element.43) | copy-start | bytes 196612
  76.1 12.2 %copy-start.34 = (f32[256,64]{0,1:T(8,128)}, f32[256,64]{0,1:T(8,128)S(1)}, u32[]{:S(2)}) copy-start(f32[256,64]{0,1:T(8,128)S(1)} %get-tuple-element.46) | copy-start | bytes 196612
  76.1 12.2 %copy-start.35 = (f32[256,64]{0,1:T(8,128)}, f32[256,64]{0,1:T(8,128)S(1)}, u32[]{:S(2)}) copy-start(f32[256,64]{0,1:T(8,128)S(1)} %get-tuple-element.47) | copy-start | bytes 196612
  97.8 11.8 %copy-start.28 = (f32[256,64]{0,1:T(8,128)}, f32[256,64]{0,1:T(8,128)S(1)}, u32[]{:S(2)}) copy-start(f32[256,64]{0,1:T(8,128)S(1)} %get-tuple-element.50) | copy-start | bytes 196612
  97.8 11.8 %copy-start.30 = (f32[256,64]{0,1:T(8,128)}, f32[256,64]{0,1:T(8,128)S(1)}, u32[]{:S(2)}) copy-start(f32[256,64]{0,1:T(8,128)S(1)} %get-tuple-element.51) | copy-start | bytes 196612
  115.3 1.0 copy-start.21
  115.3 0.9 copy-start.37
  115.4 1.2 copy-start.87
  116.5 5.3 copy-start.9
  122.7 1.0 copy-start.7
  140.6 5.6 copy-start.12
  146.6 6.6 copy-start.6
  153.9 1.0 copy-start.5
  198.5 4.6 copy-start.17
  215.2 697.3 %all-reduce.7.cloned.1.call-start = ((), (), s32[]{:S(2)}) async-start(), calls=%async_computation.3 | async-start | bytes 1048576
  502.8 2.3 copy-start.85
  504.0 1.1 copy-start.22
  505.1 12.1 %copy-start.40 = (f32[256,64]{0,1:T(8,128)}, f32[256,64]{0,1:T(8,128)S(1)}, u32[]{:S(2)}) copy-start(f32[256,64]{0,1:T(8,128)S(1)} %get-tuple-element.30) | copy-start | bytes 196612
  505.1 12.1 %copy-start.42 = (f32[256,64]{0,1:T(8,128)}, f32[256,64]{0,1:T(8,128)S(1)}, u32[]{:S(2)}) copy-start(f32[256,64]{0,1:T(8,128)S(1)} %get-tuple-element.31) | copy-start | bytes 196612
  525.2 1.8 copy-start.81
  526.4 1.0 copy-start.19
  527.0 11.8 %copy-start.32 = (f32[256,64]{0,1:T(8,128)}, f32[256,64]{0,1:T(8,128)S(1)}, u32[]{:S(2)}) copy-start(f32[256,64]{0,1:T(8,128)S(1)} %get-tuple-element.34) | copy-start | bytes 196612
  527.0 11.8 %copy-start.33 = (f32[256,64]{0,1:T(8,128)}, f32[256,64]{0,1:T(8,128)S(1)}, u32[]{:S(2)}) copy-start(f32[256,64]{0,1:T(8,128)S(1)} %get-tuple-element.35) | copy-start | bytes 196612
  546.7 2.0 copy-start.77
  548.7 11.8 %copy-start.24 = (f32[256,64]{0,1:T(8,128)}, f32[256,64]{0,1:T(8,128)S(1)}, u32[]{:S(2)}) copy-start(f32[256,64]{0,1:T(8,128)S(1)} %get-tuple-element.38) | copy-start | bytes 196612
  548.7 11.8 %copy-start.26 = (f32[256,64]{0,1:T(8,128)}, f32[256,64]{0,1:T(8,128)S(1)}, u32[]{:S(2)}) copy-start(f32[256,64]{0,1:T(8,128)S(1)} %get-tuple-element.39) | copy-start | bytes 196612
  566.2 1.0 copy-start.23
  566.2 0.9 copy-start.41
  566.2 1.2 copy-start.88
  567.4 5.1 copy-start.10
  573.3 1.0 copy-start.8
  591.4 5.4 copy-start.14
  597.2 6.5 copy-start.4
  604.5 1.0 copy-start.3
  (44 other events, 34.6 us)
Sparse Core Ops, SparseCore 0:
  215.3 253.9 all-reduce.4
  665.8 246.6 all-reduce.6
